TPU v7x, 512 devices: a whole 4x4x16 slice. The times are simulated.
512 devices in a mesh: row: 16 (over z), col: 32 (over y, x, core).
Axes of the slice: x: 4, y: 4, z: 16, core: 2. Of those that a mesh axis runs over, the one named last changes fastest.
Arguments:
- momentum: bfloat16 [8192, 28672], P('row', 'col'), may hold values from -6 to 6
- gradient: bfloat16 [8192, 28672], P('row', 'col'), may hold values from -6 to 6
- basis: bfloat16 [28672, 512], P('col'), may hold values from -6 to 6
Outputs:
- momentum_next: bfloat16 [8192, 28672], P('row', 'col')
- left_basis: float32 [8192, 512], P('row')
- right_basis: float32 [28672, 512], P('col')
All inputs are finite; a program needn't handle non-finite values.
Results may differ from a plain program's by a relative error of at most 0.013.
Values sent between devices are 32-bit elements; how exact they have to be, the bound alone decides.
A program may use at most 64 MiB of HBM per device.

v0:
```python
import jax
import jax.numpy as jnp
from jax import lax
from jax.sharding import PartitionSpec as P

decay = 0.9


def factor(gram, rows_part):
    lower = jnp.linalg.cholesky(gram)
    return jax.scipy.linalg.solve_triangular(lower, rows_part.T, lower=True).T


def shards(momentum, gradient, basis):
    buffer = (momentum.astype(jnp.float32) + gradient.astype(jnp.float32)).astype(jnp.bfloat16)
    partial_proj = jnp.dot(buffer, basis, preferred_element_type=jnp.float32)
    projected = lax.psum(partial_proj, "col")
    local_gram = jnp.dot(projected.T, projected, precision=lax.Precision.HIGHEST)
    gram = lax.psum(local_gram, "row")
    orth = factor(gram, projected)
    row_count = lax.axis_size("row") * buffer.shape[0]
    col_count = lax.axis_size("col") * buffer.shape[1]
    left_basis = jnp.sqrt(jnp.float32(row_count)) * orth
    orth_half = orth.astype(jnp.bfloat16)
    back_part = jnp.einsum("rc,rk->ck", buffer, orth_half, preferred_element_type=jnp.float32)
    back = lax.psum(back_part, "row")
    squared = jnp.sum(back * back, axis=0)
    total = lax.psum(squared, "col")
    right_basis = back * (jnp.sqrt(jnp.float32(col_count)) * lax.rsqrt(total + 1e-06))
    back_half = back.astype(jnp.bfloat16)
    update = jnp.einsum("rk,ck->rc", orth_half, back_half, preferred_element_type=jnp.float32)
    momentum_next = (buffer.astype(jnp.float32) - (1.0 - decay) * update).astype(jnp.bfloat16)
    return (momentum_next, left_basis, right_basis)


def solution(mesh):
    in_specs = (P("row", "col"), P("row", "col"), P("col", None))
    out_specs = (P("row", "col"), P("row", None), P("col", None))
    return jax.shard_map(shards, mesh=mesh, in_specs=in_specs, out_specs=out_specs, check_vma=False)
```

profile of v0, /device:TPU:1, one launch (start us, length us, event | category | flops | bytes accessed | tf_op | source)
XLA Modules:
  0.0 663.1 jit_solution(6475619407104669912)
XLA Ops:
  7.2 1.1 copy-done
  8.3 3.1 fusion.35
  11.6 141.1 %all-reduce.5.cloned.1.call-done = f32[512,512]{1,0:T(8,128)} async-done(((f32[512,512]{1,0:T(8,128)}), f32[512,512]{1,0:T(8,128)}) %all-reduce.5.cloned.1.call-update) | async-done | bytes 1048592 | tf_op jit(solution)/shard_map/psum | solution.py:17
  152.7 4.4 fusion.37
  157.1 0.5 all-reduce.9.cloned.1.call-start
  157.6 128.7 %all-reduce.7.cloned.1.call-done = f32[512,512]{0,1:T(8,128)} async-done(((f32[512,512]{0,1:T(8,128)}), f32[512,512]{0,1:T(8,128)}) %all-reduce.7.cloned.1.call-update) | async-done | bytes 1048592 | tf_op jit(solution)/shard_map/psum | solution.py:19
  286.4 1.6 copy.7
  288.3 1.0 copy-done.7
  289.2 11.7 %cholesky.104 = f32[128,128]{1,0:T(8,128)S(1)} custom-call(f32[128,128]{1,0:T(8,128)S(1)} %cholesky.266), custom_call_target="Cholesky" | custom-call | tf_op jit(solution)/shard_map/jit(cholesky)/cholesky | solution.py:10
  301.1 9.8 %custom-call.31 = f32[1,128,128]{1,2,0:T(8,128)S(1)} custom-call(f32[1,128,128]{2,1,0:T(8,128)S(1)} %get-tuple-element.33), custom_call_target="InvertDiagBlocksLowerTriangular" | custom-call | tf_op jit(solution)/shard_map/jit(cholesky)/cholesky | solution.py:10
  310.9 1.2 constant_dynamic-update-slice_fusion.3
  312.2 1.3 convolution_subtract_fusion.3
  313.5 11.7 %cholesky.217 = f32[128,128]{1,0:T(8,128)S(1)} custom-call(f32[128,128]{1,0:T(8,128)S(1)} %cholesky.270), custom_call_target="Cholesky" | custom-call | tf_op jit(solution)/shard_map/jit(cholesky)/cholesky | solution.py:10
  325.2 10.0 %custom-call.32 = f32[1,128,128]{1,2,0:T(8,128)S(1)} custom-call(f32[1,128,128]{2,1,0:T(8,128)S(1)} %get-tuple-element.30), custom_call_target="InvertDiagBlocksLowerTriangular" | custom-call | tf_op jit(solution)/shard_map/jit(cholesky)/cholesky | solution.py:10
  335.2 0.3 convolution_dynamic-update-slice_fusion
  335.4 1.3 convolution_subtract_fusion.4
  336.7 11.7 %cholesky.238 = f32[128,128]{1,0:T(8,128)S(1)} custom-call(f32[128,128]{1,0:T(8,128)S(1)} %cholesky.275), custom_call_target="Cholesky" | custom-call | tf_op jit(solution)/shard_map/jit(cholesky)/cholesky | solution.py:10
  348.5 9.8 %custom-call.33 = f32[1,128,128]{1,2,0:T(8,128)S(1)} custom-call(f32[1,128,128]{2,1,0:T(8,128)S(1)} %get-tuple-element.27), custom_call_target="InvertDiagBlocksLowerTriangular" | custom-call | tf_op jit(solution)/shard_map/jit(cholesky)/cholesky | solution.py:10
  358.5 1.2 convolution_subtract_fusion.5
  359.7 11.7 %cholesky.255 = f32[128,128]{1,0:T(8,128)S(1)} custom-call(f32[128,128]{1,0:T(8,128)S(1)} %convolution_subtract_fusion.5), custom_call_target="Cholesky" | custom-call | tf_op jit(solution)/shard_map/jit(cholesky)/cholesky | solution.py:10
  371.5 0.7 compare_reduce_fusion.1
  372.2 0.6 compare_reduce_fusion
  372.8 0.6 compare_reduce_fusion.2
  376.0 1.3 select_select_fusion
  377.3 12.0 %while.1 = (s32[]{:T(128)}, f32[512,512]{1,0:T(8,128)}, s32[4,2]{0,1:T(2,128)S(1)}, f32[4,128,128]{2,1,0:T(8,128)S(1)}, s32[]{:T(128)}) while((s32[]{:T(128)}, f32[512,512]{1,0:T(8,128)}, s32[4,2]{0,1:T(2,128)S(1)}, f32[4,128,128]{2,1,0:T(8,128)S(1)}, s32[]{:T(128)}) %tuple.32), condition=%wide.while_cond, body=%wide.while_body.sunk | while | flops 2 | bytes 131189 | solution.py:11
  377.4 0.6 fusion.47
  378.0 2.3 bitcast_dynamic-update-slice_fusion.2
  380.4 0.6 fusion.47
  381.0 2.3 bitcast_dynamic-update-slice_fusion.2
  383.5 0.6 fusion.47
  384.1 2.3 bitcast_dynamic-update-slice_fusion.2
  386.5 0.6 fusion.47
  387.1 2.3 bitcast_dynamic-update-slice_fusion.2
  389.4 39.3 %custom-call.34 = f32[4,128,128]{1,2,0:T(8,128)S(1)} custom-call(f32[4,128,128]{2,1,0:T(8,128)S(1)} %get-tuple-element.10), custom_call_target="InvertDiagBlocksLowerTriangular" | custom-call | tf_op jit(solution)/shard_map/jit(_solve_triangular)/triangular_solve | solution.py:11
  428.7 0.4 fusion.11
  429.1 1.4 convolution_subtract_fusion.1
  430.6 0.4 fusion.24
  431.0 2.0 convolution_subtract_fusion
  433.1 0.4 fusion.22
  433.5 2.4 convolution_subtract_fusion.2
  435.9 0.4 fusion.21
  436.3 1.9 fusion.33
  438.4 1.3 copy.8
  439.7 138.4 %all-reduce.9.cloned.1.call-done = f32[896,512]{1,0:T(8,128)} async-done(((f32[896,512]{1,0:T(8,128)}), f32[896,512]{1,0:T(8,128)}) %all-reduce.9.cloned.1.call-update) | async-done | bytes 1835024 | tf_op jit(solution)/shard_map/psum | solution.py:26
  578.1 1.8 multiply_reduce_fusion
  579.9 71.8 %psum.31 = f32[512]{0:T(512)S(1)} all-reduce(f32[512]{0:T(512)S(1)} %multiply_reduce_fusion), channel_id=1, replica_groups=mesh['row'=16,'col'=32] {'col'}, use_global_device_ids=true, to_apply=%region_12.13 | all-reduce | flops 512 | bytes 4096 | tf_op jit(solution)/shard_map/psum | solution.py:28
  651.7 3.2 subtract_convert_fusion
  654.9 1.4 broadcast_multiply_fusion
  (38 shorter events, 1.3 us)
Async XLA Ops:
  7.2 1.2 copy-start
  7.2 145.5 %all-reduce.5.cloned.1.call-start = ((), (), s32[]{:S(2)}) async-start(), calls=%async_computation | async-start | bytes 2097152 | tf_op jit(solution)/shard_map/psum | solution.py:17
  11.5 274.8 %all-reduce.7.cloned.1.call-start = ((), (), s32[]{:S(2)}) async-start(), calls=%async_computation.1 | async-start | bytes 2097152 | tf_op jit(solution)/shard_map/psum | solution.py:19
  157.1 421.0 %all-reduce.9.cloned.1.call-start = ((), (), s32[]{:S(2)}) async-start(), calls=%async_computation.2 | async-start | bytes 3670016 | tf_op jit(solution)/shard_map/psum | solution.py:26
  286.4 1.7 copy-start.3
  288.2 1.0 copy-start.7
  348.5 80.2 %copy-start.2 = (f32[512,512]{1,0:T(8,128)S(1)}, f32[512,512]{1,0:T(8,128)}, u32[]{:S(2)}) copy-start(f32[512,512]{1,0:T(8,128)} %all-reduce.5.cloned.1.call-done) | copy-start | bytes 3145732
  431.0 5.3 copy-start.5
  431.0 5.3 copy-start.6
  436.3 3.4 copy-start.4
  578.1 73.6 %copy-start.1 = (f32[896,512]{1,0:T(8,128)S(1)}, f32[896,512]{1,0:T(8,128)}, u32[]{:S(2)}) copy-start(f32[896,512]{1,0:T(8,128)} %all-reduce.9.cloned.1.call-done) | copy-start | bytes 5505028
Sparse Core Ops, SparseCore 0:
  11.8 140.8 all-reduce.4
  157.2 129.1 all-reduce.6
  438.4 139.6 all-reduce.8
where the time goes:
time: 667 us; the launch traced here: 663 us
  waiting for transfers between devices  408 us (61%)
  other arithmetic  123 us (18%)
  blocking collectives  71.8 us (11%)
  matrix products  25.7 us (4%)
  local copies, waits for them, and re-layouts  17.2 us (3%)
  between operations  16.8 us (3%)
    psum x1, waiting for transfers between devices, shards(): projected = lax.psum(partial_proj, 'col')  141 us
    psum x1, waiting for transfers between devices, shards(): back = lax.psum(back_part, 'row')  138 us
    psum x1, waiting for transfers between devices, shards(): gram = lax.psum(local_gram, 'row')  129 us
    another operation x14, other arithmetic, factor(): lower = jnp.linalg.cholesky(gram)  78.5 us
    psum x1, blocking collectives, shards(): total = lax.psum(squared, 'col')  71.8 us
    another operation x3, other arithmetic, factor(): return jax.scipy.linalg.solve_triangular(lower, rows_part.T, lower=True).T  40.6 us
  transfers between devices with their start and end apart: 3, of which 3 were waited for; matrix products, arithmetic and copies ran while one was open for 0% of the time, Pallas kernels for 0%

commit v1 on v0

v1 whole, which is shorter than its diff:
```python
import jax
import jax.numpy as jnp
from jax import lax
from jax.experimental import pallas as pl
from jax.experimental.pallas import tpu as pltpu
from jax.sharding import PartitionSpec as P

F32 = jnp.float32
BF16 = jnp.bfloat16
MESH = pl.DeviceIdType.MESH
decay = 0.9

NZ, NY, NX = 16, 4, 4
CHIPS = NY * NX
ROWS_L, COLS_L, RANK = 512, 896, 512
CH = 4
LW = RANK // CH
SH = COLS_L // NZ
HALF = ROWS_L // 2
PIECE = HALF // CHIPS
BLOCKS = [(i, j) for i in range(4) for j in range(i + 1)]
TILES = 16 * len(BLOCKS)
OWN = TILES // (2 * CHIPS)
NN = ((1,), (0,))
NT = ((1,), (1,))
TN = ((0,), (0,))


def dot1(a, b, dims):
    return lax.dot_general(a, b, (dims, ((), ())), preferred_element_type=F32)


def doth(a, b, dims):
    return lax.dot_general(a, b, (dims, ((), ())), preferred_element_type=F32, precision=lax.Precision.HIGHEST)


def split(a):
    high = a.astype(BF16)
    return high, (a - high.astype(F32)).astype(BF16)


def splat(a, row, lane):
    return jnp.broadcast_to(a[row : row + 1, lane : lane + 1], (8, 128))


def leaf(a_ref, w_ref, t):
    c0 = 8 * t
    ra = [jnp.broadcast_to(a_ref[c0 + i : c0 + i + 1, :], (8, 128)) for i in range(8)]
    s = {(i, j): jnp.broadcast_to(ra[i][:, c0 + j : c0 + j + 1], (8, 128)) for j in range(8) for i in range(j, 8)}
    rw = [jnp.broadcast_to(w_ref[c0 + i : c0 + i + 1, :], (8, 128)) for i in range(8)]
    low = {}
    r = []
    for k in range(8):
        rk = lax.rsqrt(s[k, k])
        r.append(rk)
        ra[k] = ra[k] * rk
        rw[k] = rw[k] * rk
        for i in range(k + 1, 8):
            low[i, k] = s[i, k] * rk
        for j in range(k + 1, 8):
            for i in range(j, 8):
                s[i, j] = s[i, j] - low[i, k] * low[j, k]
        for i in range(k + 1, 8):
            ra[i] = ra[i] - low[i, k] * ra[k]
            rw[i] = rw[i] - low[i, k] * rw[k]
    sub = lax.broadcasted_iota(jnp.int32, (8, 128), 0)
    wt = rw[0]
    for k in range(1, 8):
        wt = jnp.where(sub == k, rw[k], wt)
    for k in range(7, -1, -1):
        ra[k] = ra[k] * r[k]
        rw[k] = rw[k] * r[k]
        for i in range(k):
            ra[i] = ra[i] - low[k, i] * ra[k]
            rw[i] = rw[i] - low[k, i] * rw[k]
    for i in range(t + 1, 16):
        q = slice(8 * i, 8 * i + 8)
        ai = a_ref[q, :]
        ua = uw = None
        for j in range(8):
            m = jnp.broadcast_to(ai[:, c0 + j : c0 + j + 1], (8, 128))
            ua = m * ra[j] if j == 0 else ua + m * ra[j]
            uw = m * rw[j] if j == 0 else uw + m * rw[j]
        a_ref[q, :] = ai - ua
        w_ref[q, :] = w_ref[q, :] - uw
    w_ref[c0 : c0 + 8, :] = wt


def kernel(
    m_hbm, g_hbm, q_hbm, mom_out, left_out, right_out,
    mv, gv, qv, buf, mt, pp, sibr, rsr, pf, ph, plo, bp,
    rr, rl, bfull, bh, bl, gl, gr, gt, g, li, wd, lh, ll, lf, oh, back, nsq, nr, mn,
    in_s, out_s, s1s, s1r, s2s, s2r, s3s, s3r, s4s, s4r,
    gzs, gzr, gbs, gbr, gps, gpr, gss, gsr,
    ring_s, rsem_r, rsem_l, asem_r, asem_l, ns, nrs,
):
    z = lax.axis_index("row")
    c = lax.axis_index("col")
    y, x, k = c // 8, (c // 2) % 4, c % 2
    chip = y * NX + x
    mine = k * CHIPS + chip

    def dev(zz, yy, xx, kk):
        return (zz, (yy * NX + xx) * 2 + kk)

    def plane(dy, dx, kk):
        return dev(z, (y + dy) % NY, (x + dx) % NX, kk)

    def peer_chip(dy, dx):
        return ((y + dy) % NY) * NX + (x + dx) % NX

    offs = [(dy, dx) for dy in range(NY) for dx in range(NX) if dy or dx]
    sib = dev(z, y, x, 1 - k)
    right_dev = dev((z + 1) % NZ, y, x, k)
    left_dev = dev((z + NZ - 1) % NZ, y, x, k)

    def rcopy(src, dst, ss, rs, device):
        cp = pltpu.make_async_remote_copy(
            src_ref=src, dst_ref=dst, send_sem=ss, recv_sem=rs, device_id=device, device_id_type=MESH
        )
        cp.start()

    def wait_for(ref, sem):
        pltpu.make_async_copy(ref, ref, sem).wait()

    loads = [pltpu.make_async_copy(a, b, in_s.at[i]) for i, (a, b) in enumerate([(m_hbm, mv), (g_hbm, gv), (q_hbm, qv)])]
    for cp in loads:
        cp.start()

    bar = pltpu.get_barrier_semaphore()
    pl.semaphore_signal(bar, inc=1, device_id=sib, device_id_type=MESH)
    for dy, dx in offs:
        for kk in range(2):
            pl.semaphore_signal(bar, inc=1, device_id=plane(dy, dx, kk), device_id_type=MESH)
    for dz in range(1, NZ):
        pl.semaphore_signal(bar, inc=1, device_id=dev((z + dz) % NZ, y, x, k), device_id_type=MESH)

    loads[0].wait()
    loads[1].wait()
    for r in range(4):
        rows = pl.ds(128 * r, 128)
        buf[rows, :] = (mv[rows, :].astype(F32) + gv[rows, :].astype(F32)).astype(BF16)
    loads[2].wait()
    for h in range(2):
        part = dot1(buf[...], qv[:, 256 * h : 256 * h + 256], NN)
        pp[2 * h] = part[:, :128]
        pp[2 * h + 1] = part[:, 128:]

    pl.semaphore_wait(bar, 31 + NZ - 1)

    my_half = pl.multiple_of(HALF * k, HALF)
    other_half = pl.multiple_of(HALF * (1 - k), HALF)
    my_piece = pl.multiple_of(HALF * k + PIECE * chip, PIECE)
    for q in range(CH):
        rcopy(pp.at[q, pl.ds(other_half, HALF)], sibr.at[q], s1s.at[q], s1r.at[q], sib)
    for r in range(4):
        mt[:, 128 * r : 128 * r + 128] = buf[128 * r : 128 * r + 128, :].T
    for q in range(CH):
        wait_for(sibr.at[q], s1r.at[q])
        rows = pl.ds(my_half, HALF)
        pp[q, rows, :] = pp[q, rows, :] + sibr[q]
        for n, (dy, dx) in enumerate(offs):
            piece = pl.multiple_of(HALF * k + PIECE * peer_chip(dy, dx), PIECE)
            rcopy(pp.at[q, pl.ds(piece, PIECE)], rsr.at[q, n], s2s.at[q], s2r.at[q], plane(dy, dx, k))
    for q in range(CH):
        wait_for(rsr.at[q], s2r.at[q])
        rows = pl.ds(my_piece, PIECE)
        total = pp[q, rows, :]
        for n in range(CHIPS - 1):
            total = total + rsr[q, n]
        pf[q, rows, :] = total
        for n, (dy, dx) in enumerate(offs):
            rcopy(pf.at[q, rows], pf.at[q, rows], s3s.at[q], s3r.at[q], plane(dy, dx, k))
    for q in range(CH):
        wait_for(rsr.at[q], s3r.at[q])
        half = pf.at[q, pl.ds(my_half, HALF)]
        rcopy(half, half, s4s.at[q], s4r.at[q], sib)

    def shard(i):
        return pl.ds(pl.multiple_of(SH * lax.rem(i + 2 * NZ, NZ), 8), SH)

    def ring(q, e):
        if e == 0:
            rcopy(bp.at[q, shard(z + 8)], rr.at[q, 0], ring_s.at[q, 0], rsem_r.at[q, 0], right_dev)
            rcopy(bp.at[q, shard(z - 7)], rl.at[q, 0], ring_s.at[q, 1], rsem_l.at[q, 0], left_dev)
        elif e < 8:
            wait_for(rr.at[q, e - 1], rsem_r.at[q, e - 1])
            rr[q, e - 1] = rr[q, e - 1] + bp[q, shard(z + 8 - e), :]
            rcopy(rr.at[q, e - 1], rr.at[q, e], ring_s.at[q, 0], rsem_r.at[q, e], right_dev)
            wait_for(rl.at[q, e - 1], rsem_l.at[q, e - 1])
            if e < 7:
                rl[q, e - 1] = rl[q, e - 1] + bp[q, shard(z - 7 + e), :]
                rcopy(rl.at[q, e - 1], rl.at[q, e], ring_s.at[q, 1], rsem_l.at[q, e], left_dev)
        elif e == 8:
            wait_for(rr.at[q, 7], rsem_r.at[q, 7])
            own = shard(z)
            bfull[q, own, :] = bp[q, own, :] + rl[q, 6] + rr[q, 7]
            blk = bfull.at[q, own]
            rcopy(blk, blk, ring_s.at[q, 0], asem_r.at[q, 0], right_dev)
            rcopy(blk, blk, ring_s.at[q, 1], asem_l.at[q, 0], left_dev)
        else:
            n = e - 9
            blk = bfull.at[q, shard(z - 1 - n)]
            wait_for(blk, asem_r.at[q, n])
            if e < 16:
                rcopy(blk, blk, ring_s.at[q, 0], asem_r.at[q, n + 1], right_dev)
                blk = bfull.at[q, shard(z + 1 + n)]
                wait_for(blk, asem_l.at[q, n])
                if e < 15:
                    rcopy(blk, blk, ring_s.at[q, 1], asem_l.at[q, n + 1], left_dev)

    for q in range(CH):
        wait_for(sibr.at[q], s4r.at[q])
        high, low = split(pf[q])
        cols = slice(LW * q, LW * q + LW)
        ph[:, cols] = high
        plo[:, cols] = low
        both = jnp.concatenate([high, low], axis=1)
        for r in range(7):
            rows = pl.ds(128 * r, 128)
            part = dot1(mt[rows, :], both, NN)
            bp[q, rows, :] = part[:, :128] + part[:, 128:]
        ring(q, 0)

    owner = jnp.logical_and(z % 3 == 0, z < 15)
    my_u = lax.rem(z // 3, OWN)
    my_tiles = OWN * mine

    def chol():
        for b, (i, j) in enumerate(BLOCKS):
            gl[b * 16 : b * 16 + 16] = doth(pf[i], pf[j], TN).reshape(16, 8, 128)
        for u in range(OWN):
            @pl.when(z != 3 * u)
            def _():
                rcopy(gl.at[my_tiles + u], gr.at[z], gzs, gzr, dev(3 * u, y, x, k))
        yield
        @pl.when(owner)
        def _():
            wait_for(gr.at[pl.ds(0, NZ - 1)], gzr)
            gr[z] = gl[my_tiles + my_u]
            total = gr[0]
            for n in range(1, NZ):
                total = total + gr[n]
            dst = gt.at[my_tiles + my_u]
            gt[my_tiles + my_u] = total
            for dz in range(1, NZ):
                rcopy(dst, dst, gbs, gbr, dev((z + dz) % NZ, y, x, k))
        yield
        own = gt.at[pl.ds(my_tiles, OWN)]
        @pl.when(owner)
        def _():
            wait_for(gt.at[pl.ds(0, OWN - 1)], gbr)
        @pl.when(jnp.logical_not(owner))
        def _():
            wait_for(gt.at[pl.ds(0, OWN)], gbr)
        for n, (dy, dx) in enumerate(offs):
            rcopy(own, own, gps, gpr, plane(dy, dx, k))
        yield
        wait_for(gt.at[pl.ds(0, OWN * (CHIPS - 1))], gpr)
        half = gt.at[pl.ds(OWN * CHIPS * k, OWN * CHIPS)]
        rcopy(half, half, gss, gsr, sib)
        yield
        wait_for(gt.at[pl.ds(0, OWN * CHIPS)], gsr)
        for b, (i, j) in enumerate(BLOCKS):
            g[128 * i : 128 * i + 128, 128 * j : 128 * j + 128] = gt[16 * b : 16 * b + 16].reshape(128, 128)
        yield
        eye = lax.broadcasted_iota(jnp.int32, (128, 128), 0) == lax.broadcasted_iota(jnp.int32, (128, 128), 1)
        for kb in range(4):
            K = slice(128 * kb, 128 * kb + 128)
            before = slice(0, 128 * kb)
            wd[...] = eye.astype(F32)
            for t in range(16):
                leaf(g.at[K, K], wd, t)
                yield
            w = wd[...]
            li[K, K] = w
            if kb:
                li[K, before] = doth(w, li[K, before], NN)
            if kb < 3:
                R = slice(128 * (kb + 1), 512)
                lp = doth(g[R, K], w, NT)
                g[R, R] = g[R, R] - doth(lp, lp, NT)
                yield
                if kb:
                    li[R, before] = li[R, before] - doth(lp, li[K, before], NN)
                li[R, K] = -doth(lp, w, NN)
                li[K, 128 * (kb + 1) :] = jnp.zeros((128, 512 - 128 * (kb + 1)), F32)
            yield
        lh[...], ll[...] = split(li[...])
        yield
        for j in range(4):
            K = 128 * (j + 1)
            J = slice(128 * j, 128 * j + 128)
            a, b = lh[J, :K], ll[J, :K]
            orth = dot1(ph[:, :K], a, NT) + (dot1(ph[:, :K], b, NT) + dot1(plo[:, :K], a, NT))
            oh[:, J] = orth.astype(BF16)
            lf[:, J] = jnp.sqrt(F32(NZ * ROWS_L)) * orth
            yield
        pltpu.make_async_copy(lf, left_out, out_s.at[0]).start()
        yield

    work = chol()
    done = object()

    def pull(n):
        for _ in range(n):
            next(work, done)

    pull(1)
    for e in range(1, 16):
        for q in range(CH):
            ring(q, e)
            if e <= 4:
                if q == CH - 1:
                    pull(1)
            else:
                pull(2)
    while next(work, done) is not done:
        pass

    for q in range(CH):
        ring(q, 16)
        J = slice(128 * q, 128 * q + 128)
        bh[:, J], bl[:, J] = split(bfull[q])
        K = 128 * (q + 1)
        a, b = lh[J, :K], ll[J, :K]
        part = dot1(bh[:, :K], a, NT) + (dot1(bh[:, :K], b, NT) + dot1(bl[:, :K], a, NT))
        back[:, J] = part
        nsq[q : q + 1, :] = jnp.sum(part * part, axis=0, keepdims=True)
    nsq[4:8, :] = jnp.zeros((4, 128), F32)
    rcopy(nsq, nr.at[0], ns, nrs, sib)
    for n, (dy, dx) in enumerate(offs):
        for kk in range(2):
            rcopy(nsq, nr.at[1 + 2 * n + kk], ns, nrs, plane(dy, dx, jnp.where(kk == 0, k, 1 - k)))

    for r in range(4):
        rows = slice(128 * r, 128 * r + 128)
        for cc in range(7):
            cols = slice(128 * cc, 128 * cc + 128)
            update = dot1(oh[rows, :], back[cols, :].astype(BF16), NT)
            mn[rows, cols] = (buf[rows, cols].astype(F32) - F32(1.0 - decay) * update).astype(BF16)
    out_mom = pltpu.make_async_copy(mn, mom_out, out_s.at[1])
    out_mom.start()

    wait_for(nr.at[pl.ds(0, 31)], nrs)
    total = nsq[...]
    for n in range(31):
        total = total + nr[n]
    scale = jnp.sqrt(F32(2 * CHIPS * COLS_L)) * lax.rsqrt(total + 1e-06)
    for q in range(CH):
        J = slice(128 * q, 128 * q + 128)
        back[:, J] = back[:, J] * scale[q : q + 1, :]
    out_right = pltpu.make_async_copy(back, right_out, out_s.at[2])
    out_right.start()

    for q in range(CH):
        wait_for(sibr.at[q], s1s.at[q])
        wait_for(rsr.at[q], s2s.at[q])
        wait_for(rsr.at[q], s3s.at[q])
        wait_for(sibr.at[q], s4s.at[q])
        for _ in range(2):
            wait_for(rr.at[q], ring_s.at[q, 0])
            wait_for(rl.at[q], ring_s.at[q, 1])

    @pl.when(owner)
    def _():
        wait_for(gt.at[pl.ds(0, OWN - 1)], gzs)
        wait_for(gt.at[pl.ds(0, NZ - 1)], gbs)

    @pl.when(jnp.logical_not(owner))
    def _():
        wait_for(gt.at[pl.ds(0, OWN)], gzs)

    wait_for(gt.at[pl.ds(0, OWN * (CHIPS - 1))], gps)
    wait_for(gt.at[pl.ds(0, OWN * CHIPS)], gss)
    wait_for(nr.at[pl.ds(0, 31)], ns)
    pltpu.make_async_copy(lf, left_out, out_s.at[0]).wait()
    out_mom.wait()
    out_right.wait()


def shards(momentum, gradient, basis):
    V = pltpu.VMEM
    D = pltpu.SemaphoreType.DMA
    scratch = [
        V((512, 896), BF16), V((512, 896), BF16), V((896, 512), BF16),
        V((512, 896), BF16), V((896, 512), BF16),
        V((CH, 512, 128), F32), V((CH, HALF, 128), F32), V((CH, CHIPS - 1, PIECE, 128), F32),
        V((CH, 512, 128), F32), V((512, 512), BF16), V((512, 512), BF16), V((CH, 896, 128), F32),
        V((CH, 8, SH, 128), F32), V((CH, 7, SH, 128), F32), V((CH, 896, 128), F32),
        V((896, 512), BF16), V((896, 512), BF16),
        V((TILES, 8, 128), F32), V((NZ, 8, 128), F32), V((TILES, 8, 128), F32),
        V((512, 512), F32), V((512, 512), F32), V((128, 128), F32),
        V((512, 512), BF16), V((512, 512), BF16), V((512, 512), F32), V((512, 512), BF16),
        V((896, 512), F32), V((8, 128), F32), V((31, 8, 128), F32), V((512, 896), BF16),
        D((3,)), D((3,)), D((CH,)), D((CH,)), D((CH,)), D((CH,)), D((CH,)), D((CH,)), D((CH,)), D((CH,)),
        D, D, D, D, D, D, D, D,
        D((CH, 2)), D((CH, 8)), D((CH, 7)), D((CH, 8)), D((CH, 7)), D, D,
    ]
    return pl.pallas_call(
        kernel,
        name="dion",
        out_shape=(
            jax.ShapeDtypeStruct((512, 896), BF16),
            jax.ShapeDtypeStruct((512, 512), F32),
            jax.ShapeDtypeStruct((896, 512), F32),
        ),
        in_specs=[pl.BlockSpec(memory_space=pl.ANY)] * 3,
        out_specs=[pl.BlockSpec(memory_space=pl.ANY)] * 3,
        scratch_shapes=scratch,
        compiler_params=pltpu.CompilerParams(
            collective_id=0, has_side_effects=True, vmem_limit_bytes=50 * 2**20
        ),
    )(momentum, gradient, basis)


def solution(mesh):
    in_specs = (P("row", "col"), P("row", "col"), P("col", None))
    out_specs = (P("row", "col"), P("row", None), P("col", None))
    return jax.shard_map(shards, mesh=mesh, in_specs=in_specs, out_specs=out_specs, check_vma=False)
```

time: 667 us -> 120 us (0.18)
  waiting for transfers between devices: 408 us -> 0 us
  other arithmetic: 123 us -> 0 us
  Pallas kernels: 0 us -> 112 us
  blocking collectives: 71.8 us -> 0 us
  matrix products: 25.7 us -> 0 us
  between operations: 16.8 us -> 0.67 us
  local copies, waits for them, and re-layouts: 17.2 us -> 7.27 us
    psum x3 -> x0, waiting for transfers between devices: 408 us -> none  [the longest x1 141 us: shards(): projected = lax.psum(partial_proj, 'col')]
    another operation x17 -> x0, other arithmetic: 119 us -> none  [the longest x14 78.5 us: factor(): lower = jnp.linalg.cholesky(gram)]
    pallas_call x0 -> x1, Pallas kernels: none -> 112 us  [shards(): pl.pallas_call(kernel, name='dion', out_shape=(jax.ShapeDtypeStruct((512,...]
    psum x1 -> x0, blocking collectives: 71.8 us -> none  [shards(): total = lax.psum(squared, 'col')]
    another operation x13 -> x0, matrix products: 13 us -> none  [the longest x7 7.53 us: factor(): return jax.scipy.linalg.solve_triangular(lower, rows_part.T, lower=True).T]
    dot_general x4 -> x0, matrix products: 12.7 us -> none  [the longest x1 4.39 us: shards(): jnp.dot(projected.T, projected, precision=lax.Precision.HIGHEST)]
    another operation x17 -> x0, local copies, waits for them, and re-layouts: 12.1 us -> none
  transfers between devices with their start and end apart: 3 -> 0, of which waited for: 3 -> 0; matrix products, arithmetic and copies ran while one was open for 0% -> 0% of each run, Pallas kernels for 0% -> 0%
where the time goes in v1:
time: 120 us
  Pallas kernels  112 us (93%)
  local copies, waits for them, and re-layouts  7.27 us (6%)
    pallas_call x1, Pallas kernels, shards(): pl.pallas_call(kernel, name='dion', out_shape=(jax.ShapeDtypeStruct((512,...  112 us
    unnamed x13, local copies, waits for them, and re-layouts  7.27 us

profile of v1, /device:TPU:1, one launch (start us, length us, event | category | flops | bytes accessed | tf_op | source)
XLA Modules:
  0.0 119.9 jit_solution(5283072259832522258)
XLA Ops:
  0.6 0.0 copy-start
  0.6 1.2 copy-done
  1.8 0.0 copy-start.1
  1.8 1.2 copy-done.1
  3.0 0.0 copy-start.2
  3.0 1.2 copy-done.2
  4.2 111.9 %dion.1 = (bf16[512,896]{1,0:T(8,128)(2,1)S(1)}, f32[512,512]{1,0:T(8,128)}, f32[896,512]{1,0:T(8,128)}) custom-call(bf16[512,896]{1,0:T(8,128)(2,1)S(1)} %copy-done, bf16[512,896]{1,0:T(8,128)(2,1)S(1)} %copy-done.1, bf16[896,512]{1,0:T(8,128)(2,1)S(1)} %copy-done.2), custom_call_target="tpu_custom_call" | custom-call | tf_op jit(solution)/shard_map/dion/pallas_call | solution.py:400
  116.1 0.0 copy-start.4
  116.1 0.0 copy-start.3
  116.1 0.9 copy.9
  117.1 0.6 copy-done.4
  117.7 1.0 copy.10
  118.6 0.0 copy-done.3
  118.6 1.2 %copy.11 = f32[896,512]{1,0:T(8,128)} copy(f32[896,512]{1,0:T(8,128)S(1)} %copy-done.3) | data formatting | bytes 3670016
Async XLA Ops:
  0.6 1.2 copy-start
  1.8 1.2 copy-start.1
  3.0 1.2 copy-start.2
  116.1 1.6 %copy-start.4 = (f32[512,512]{1,0:T(8,128)S(1)}, f32[512,512]{1,0:T(8,128)}, u32[]{:S(2)}) copy-start(f32[512,512]{1,0:T(8,128)} %get-tuple-element.7) | copy-start | bytes 3145732
  116.1 2.5 %copy-start.3 = (f32[896,512]{1,0:T(8,128)S(1)}, f32[896,512]{1,0:T(8,128)}, u32[]{:S(2)}) copy-start(f32[896,512]{1,0:T(8,128)} %get-tuple-element.8) | copy-start | bytes 5505028

commit v2 on v1

v2 whole, which is shorter than its diff:
```python
import jax
import jax.numpy as jnp
from jax import lax
from jax.experimental import pallas as pl
from jax.experimental.pallas import tpu as pltpu
from jax.sharding import PartitionSpec as P

F32 = jnp.float32
BF16 = jnp.bfloat16
MESH = pl.DeviceIdType.MESH
decay = 0.9

NZ, NY, NX = 16, 4, 4
CHIPS = NY * NX
ROWS_L, COLS_L, RANK = 512, 896, 512
CH = 4
LW = RANK // CH
SH = COLS_L // NZ
HALF = ROWS_L // 2
PIECE = HALF // CHIPS
BLOCKS = [(i, j) for i in range(4) for j in range(i + 1)]
TILES = 16 * len(BLOCKS)
OWN = TILES // (2 * CHIPS)
PLANS = [
    ((8, 7, 6, 5, 4, 3, 2, 0), (7, 6, 5, 4, 3, 2, 1, 0)),
    ((7, 6, 5, 4, 3, 2, 1, 0), (8, 7, 6, 5, 4, 3, 2, 0)),
    ((8, 7, 6, 5, 4, 3, 2, 0), (7, 6, 5, 4, 3, 2, 1, 0)),
    ((7, 6, 5, 4, 3, 2, 1, 0), (8, 7, 6, 5, 4, 3, 2, 0)),
]
SOLO_AT = 2
GRAM_AT = (8, 14, 21, 24)
PER_GAP = 3
NN = ((1,), (0,))
NT = ((1,), (1,))
TN = ((0,), (0,))


def dot1(a, b, dims):
    return lax.dot_general(a, b, (dims, ((), ())), preferred_element_type=F32)


def doth(a, b, dims):
    return lax.dot_general(a, b, (dims, ((), ())), preferred_element_type=F32, precision=lax.Precision.HIGHEST)


def split(a):
    high = a.astype(BF16)
    return high, (a - high.astype(F32)).astype(BF16)


def splat(a, row, lane):
    return jnp.broadcast_to(a[row : row + 1, lane : lane + 1], (8, 128))


def leaf(a_ref, w_ref, t):
    c0 = 8 * t
    ra = [jnp.broadcast_to(a_ref[c0 + i : c0 + i + 1, :], (8, 128)) for i in range(8)]
    s = {(i, j): jnp.broadcast_to(ra[i][:, c0 + j : c0 + j + 1], (8, 128)) for j in range(8) for i in range(j, 8)}
    rw = [jnp.broadcast_to(w_ref[c0 + i : c0 + i + 1, :], (8, 128)) for i in range(8)]
    low = {}
    r = []
    for k in range(8):
        rk = lax.rsqrt(s[k, k])
        r.append(rk)
        ra[k] = ra[k] * rk
        rw[k] = rw[k] * rk
        for i in range(k + 1, 8):
            low[i, k] = s[i, k] * rk
        for j in range(k + 1, 8):
            for i in range(j, 8):
                s[i, j] = s[i, j] - low[i, k] * low[j, k]
        for i in range(k + 1, 8):
            ra[i] = ra[i] - low[i, k] * ra[k]
            rw[i] = rw[i] - low[i, k] * rw[k]
    sub = lax.broadcasted_iota(jnp.int32, (8, 128), 0)
    wt = rw[0]
    for k in range(1, 8):
        wt = jnp.where(sub == k, rw[k], wt)
    for k in range(7, -1, -1):
        ra[k] = ra[k] * r[k]
        rw[k] = rw[k] * r[k]
        for i in range(k):
            ra[i] = ra[i] - low[k, i] * ra[k]
            rw[i] = rw[i] - low[k, i] * rw[k]
    for i in range(t + 1, 16):
        q = slice(8 * i, 8 * i + 8)
        ai = a_ref[q, :]
        ua = uw = None
        for j in range(8):
            m = jnp.broadcast_to(ai[:, c0 + j : c0 + j + 1], (8, 128))
            ua = m * ra[j] if j == 0 else ua + m * ra[j]
            uw = m * rw[j] if j == 0 else uw + m * rw[j]
        a_ref[q, :] = ai - ua
        w_ref[q, :] = w_ref[q, :] - uw
    w_ref[c0 : c0 + 8, :] = wt


def kernel(
    m_hbm, g_hbm, q_hbm, mn, lf, back,
    mv, gv, qv, buf, mt, pp, sibr, rsr, pf, ph, plo, bp,
    run, solo, bfull, bh, bl, gl, gr, gt, pt, g, li, wd, lh, ll, oh, bb, nsq, nr,
    in_s, s1s, s1r, s2s, s2r, s3s, s3r, s4s, s4r,
    gzs, gzr, gbs, gbr, gps, gpr, gss, gsr,
    ring_s, run_r, solo_r, all_r, skip_r, ns, nrs,
):
    z = lax.axis_index("row")
    c = lax.axis_index("col")
    y, x, k = c // 8, (c // 2) % 4, c % 2
    chip = y * NX + x
    mine = k * CHIPS + chip

    def dev(zz, yy, xx, kk):
        return (zz, (yy * NX + xx) * 2 + kk)

    def plane(dy, dx, kk):
        return dev(z, (y + dy) % NY, (x + dx) % NX, kk)

    def peer_chip(dy, dx):
        return ((y + dy) % NY) * NX + (x + dx) % NX

    offs = [(dy, dx) for dy in range(NY) for dx in range(NX) if dy or dx]
    sib = dev(z, y, x, 1 - k)

    def rcopy(src, dst, ss, rs, device):
        cp = pltpu.make_async_remote_copy(
            src_ref=src, dst_ref=dst, send_sem=ss, recv_sem=rs, device_id=device, device_id_type=MESH
        )
        cp.start()

    finals = []

    def wait_for(ref, sem):
        pltpu.make_async_copy(ref, ref, sem).wait()

    loads = [pltpu.make_async_copy(a, b, in_s.at[i]) for i, (a, b) in enumerate([(m_hbm, mv), (g_hbm, gv), (q_hbm, qv)])]
    for cp in loads:
        cp.start()

    bar = pltpu.get_barrier_semaphore()
    pl.semaphore_signal(bar, inc=1, device_id=sib, device_id_type=MESH)
    for dy, dx in offs:
        for kk in range(2):
            pl.semaphore_signal(bar, inc=1, device_id=plane(dy, dx, kk), device_id_type=MESH)
    for dz in range(1, NZ):
        pl.semaphore_signal(bar, inc=1, device_id=dev((z + dz) % NZ, y, x, k), device_id_type=MESH)

    my_half = pl.multiple_of(HALF * k, HALF)
    other_half = pl.multiple_of(HALF * (1 - k), HALF)
    my_piece = pl.multiple_of(HALF * k + PIECE * chip, PIECE)

    def project(start):
        rows = pl.ds(start, HALF)
        part = dot1(buf[rows, :], qv[...], NN)
        for q in range(CH):
            pp[q, rows, :] = part[:, LW * q : LW * q + LW]

    loads[0].wait()
    loads[1].wait()
    for r in range(4):
        rows = pl.ds(128 * r, 128)
        buf[rows, :] = (mv[rows, :].astype(F32) + gv[rows, :].astype(F32)).astype(BF16)
    loads[2].wait()
    project(other_half)

    pl.semaphore_wait(bar, 31 + NZ - 1)

    for q in range(CH):
        rcopy(pp.at[q, pl.ds(other_half, HALF)], sibr.at[q], s1s.at[q], s1r.at[q], sib)
        finals.append(lambda q=q: wait_for(sibr.at[q], s1s.at[q]))
    project(my_half)
    for q in range(CH):
        wait_for(sibr.at[q], s1r.at[q])
        rows = pl.ds(my_half, HALF)
        pp[q, rows, :] = pp[q, rows, :] + sibr[q]
        for n, (dy, dx) in enumerate(offs):
            piece = pl.multiple_of(HALF * k + PIECE * peer_chip(dy, dx), PIECE)
            rcopy(pp.at[q, pl.ds(piece, PIECE)], rsr.at[q, n], s2s.at[q], s2r.at[q], plane(dy, dx, k))
    for r in range(4):
        mt[:, 128 * r : 128 * r + 128] = buf[128 * r : 128 * r + 128, :].T
    for q in range(CH):
        finals.append(lambda q=q: wait_for(rsr.at[q], s2s.at[q]))
        finals.append(lambda q=q: wait_for(rsr.at[q], s3s.at[q]))
        wait_for(rsr.at[q], s2r.at[q])
        rows = pl.ds(my_piece, PIECE)
        total = pp[q, rows, :]
        for n in range(CHIPS - 1):
            total = total + rsr[q, n]
        pf[q, rows, :] = total
        for n, (dy, dx) in enumerate(offs):
            rcopy(pf.at[q, rows], pf.at[q, rows], s3s.at[q], s3r.at[q], plane(dy, dx, k))
    for q in range(CH):
        wait_for(rsr.at[q], s3r.at[q])
        half = pf.at[q, pl.ds(my_half, HALF)]
        rcopy(half, half, s4s.at[q], s4r.at[q], sib)
        finals.append(lambda q=q: wait_for(sibr.at[q], s4s.at[q]))

    def shard(i):
        return pl.ds(pl.multiple_of(SH * lax.rem(i + 2 * NZ, NZ), 8), SH)

    def zdev(step):
        return dev((z + step + NZ) % NZ, y, x, k)

    def ring_events(q):
        sent = [0, 0]

        def send(src, dst, way, sem, hop):
            sent[way] += 1
            rcopy(src, dst, ring_s.at[q, way], sem, zdev(hop if way == 0 else -hop))

        def at(way, dist):
            return shard(z + dist if way == 0 else z - dist)

        def finish(way):
            def fn():
                for n in range(0, sent[way], NZ):
                    wait_for(bfull.at[q, pl.ds(0, SH * min(NZ, sent[way] - n))], ring_s.at[q, way])
            return fn

        finals.append(finish(0))
        finals.append(finish(1))
        hops = [len(PLANS[q][0]) - 1, len(PLANS[q][1]) - 1]
        for way in range(2):
            stops = PLANS[q][way]
            send(bp.at[q, at(way, stops[0])], run.at[q, way, 0], way, run_r.at[q, way, 0], stops[0] - stops[1])

        def solos():
            for way in range(2):
                stops = PLANS[q][way]
                for i in range(hops[way]):
                    if stops[i] - stops[i + 1] == 2:
                        send(bp.at[q, at(way, stops[i] - 1)], solo.at[q, way, i], way, solo_r.at[q, way, i], 1)

        if SOLO_AT == 0:
            solos()
        yield

        def arrived(way, i):
            stops = PLANS[q][way]
            wait_for(run.at[q, way, i], run_r.at[q, way, i])
            total = run[q, way, i]
            if stops[i] - stops[i + 1] == 2:
                wait_for(solo.at[q, way, i], solo_r.at[q, way, i])
                total = total + solo[q, way, i]
            return total

        for i in range(1, max(hops)):
            for way in range(2):
                stops = PLANS[q][way]
                if i < hops[way]:
                    run[q, way, i - 1] = arrived(way, i - 1) + bp[q, at(way, stops[i]), :]
                    send(run.at[q, way, i - 1], run.at[q, way, i], way, run_r.at[q, way, i], stops[i] - stops[i + 1])
            if i == SOLO_AT:
                solos()
            yield
        own = shard(z)
        total = arrived(0, hops[0] - 1) + arrived(1, hops[1] - 1)
        bfull[q, own, :] = bp[q, own, :] + total

        def forward(way, i):
            stops = PLANS[q][way][::-1]
            blk = bfull.at[q, at(way, -stops[i])]
            if i:
                wait_for(blk, all_r.at[q, way, i - 1])
            if i < hops[way]:
                send(blk, blk, way, all_r.at[q, way, i], stops[i + 1] - stops[i])

        def skips(way, i):
            stops = PLANS[q][way][::-1]
            if 0 <= i < hops[way] and stops[i + 1] - stops[i] == 2:
                blk = bfull.at[q, at(way, -stops[i])]
                send(blk, blk, way, skip_r.at[q, way, i], 1)

        for i in range(max(hops) + 1):
            for way in range(2):
                if i <= hops[way]:
                    forward(way, i)
            for way in range(2):
                skips(way, i - 1)
            if i == max(hops):
                for way in range(2):
                    stops = PLANS[q][way][::-1]
                    for n in range(hops[way]):
                        if stops[n + 1] - stops[n] == 2:
                            wait_for(bfull.at[q, at(way, -stops[n] - 1)], skip_r.at[q, way, n])
            yield

    events = []
    for q in range(CH):
        wait_for(sibr.at[q], s4r.at[q])
        high, low = split(pf[q])
        cols = slice(LW * q, LW * q + LW)
        ph[:, cols] = high
        plo[:, cols] = low
        both = jnp.concatenate([high, low], axis=1)
        for r in range(7):
            rows = pl.ds(128 * r, 128)
            part = dot1(mt[rows, :], both, NN)
            bp[q, rows, :] = part[:, :128] + part[:, 128:]
        events.append(ring_events(q))
        next(events[q])
        pt[cols, :] = pf[q].T

    my_u = (z % 8) * 3 % 8
    owner = my_u < OWN
    my_u = my_u % OWN
    my_tiles = OWN * mine

    def chol():
        for u in range(OWN):
            tile = my_tiles + u
            b = tile // 16
            i = (b + 9) // 10 + (b + 7) // 10 + (b + 4) // 10
            j = b - i * (i + 1) // 2
            lhs = pt[pl.ds(pl.multiple_of(128 * i + 8 * (tile % 16), 8), 8), :]
            gl[u] = doth(lhs, pf[j], NN)
        for u in range(OWN):
            for far in (0, 8):
                at_z = (3 * u + far) % NZ

                @pl.when(z != at_z)
                def _():
                    rcopy(gl.at[u], gr.at[z], gzs, gzr, dev(at_z, y, x, k))

        def f1():
            @pl.when(owner)
            def _():
                wait_for(gt.at[pl.ds(0, 2 * OWN - 1)], gzs)
                wait_for(gt.at[pl.ds(0, 7)], gbs)

            @pl.when(jnp.logical_not(owner))
            def _():
                wait_for(gt.at[pl.ds(0, 2 * OWN)], gzs)

        finals.append(f1)
        finals.append(lambda: wait_for(gt.at[pl.ds(0, OWN * (CHIPS - 1))], gps))
        finals.append(lambda: wait_for(gt.at[pl.ds(0, OWN * CHIPS)], gss))
        yield
        @pl.when(owner)
        def _():
            wait_for(gr.at[pl.ds(0, NZ - 1)], gzr)
            gr[z] = gl[my_u]
            total = gr[0]
            for n in range(1, NZ):
                total = total + gr[n]
            dst = gt.at[my_tiles + my_u]
            gt[my_tiles + my_u] = total
            for dz in (1, -1, 2, -2, 3, -3, 4):
                rcopy(dst, dst, gbs, gbr, dev((z + dz + NZ) % NZ, y, x, k))
        yield
        own = gt.at[pl.ds(my_tiles, OWN)]
        @pl.when(owner)
        def _():
            wait_for(gt.at[pl.ds(0, OWN - 1)], gbr)
        @pl.when(jnp.logical_not(owner))
        def _():
            wait_for(gt.at[pl.ds(0, OWN)], gbr)
        for n, (dy, dx) in enumerate(offs):
            rcopy(own, own, gps, gpr, plane(dy, dx, k))
        yield
        wait_for(gt.at[pl.ds(0, OWN * (CHIPS - 1))], gpr)
        half = gt.at[pl.ds(OWN * CHIPS * k, OWN * CHIPS)]
        rcopy(half, half, gss, gsr, sib)
        yield
        wait_for(gt.at[pl.ds(0, OWN * CHIPS)], gsr)
        for b, (i, j) in enumerate(BLOCKS):
            g[128 * i : 128 * i + 128, 128 * j : 128 * j + 128] = gt[16 * b : 16 * b + 16].reshape(128, 128)
        yield
        eye = lax.broadcasted_iota(jnp.int32, (128, 128), 0) == lax.broadcasted_iota(jnp.int32, (128, 128), 1)
        for kb in range(4):
            K = slice(128 * kb, 128 * kb + 128)
            before = slice(0, 128 * kb)
            wd[...] = eye.astype(F32)
            for t in range(16):
                leaf(g.at[K, K], wd, t)
                yield
            w = wd[...]
            li[K, K] = w
            if kb:
                li[K, before] = doth(w, li[K, before], NN)
            if kb < 3:
                R = slice(128 * (kb + 1), 512)
                lp = doth(g[R, K], w, NT)
                g[R, R] = g[R, R] - doth(lp, lp, NT)
                yield
                if kb:
                    li[R, before] = li[R, before] - doth(lp, li[K, before], NN)
                li[R, K] = -doth(lp, w, NN)
                li[K, 128 * (kb + 1) :] = jnp.zeros((128, 512 - 128 * (kb + 1)), F32)
            yield
        lh[...], ll[...] = split(li[...])
        yield

    work = chol()
    done = object()

    def pull(n):
        for _ in range(n):
            next(work, done)

    pull(1)
    last = max(len(p) - 1 for plan in PLANS for p in plan) * 2
    count = 0
    for e in range(1, last + 1):
        for q in range(CH):
            if next(events[q], done) is done:
                continue
            count += 1
            if count in GRAM_AT:
                pull(1)
            elif count > GRAM_AT[-1]:
                pull(PER_GAP)
    while next(work, done) is not done:
        pass

    for q in range(CH):
        J = slice(128 * q, 128 * q + 128)
        bh[:, J], bl[:, J] = split(bfull[q])
    for h in range(2):
        J = slice(256 * h, 256 * h + 256)
        K = 256 * (h + 1)
        a, b = lh[J, :K], ll[J, :K]
        part = dot1(bh[:, :K], a, NT) + (dot1(bh[:, :K], b, NT) + dot1(bl[:, :K], a, NT))
        back[:, J] = part
        bb[:, J] = part.astype(BF16)
        sq = jnp.sum(part * part, axis=0, keepdims=True)
        nsq[2 * h : 2 * h + 1, :] = sq[:, :128]
        nsq[2 * h + 1 : 2 * h + 2, :] = sq[:, 128:]
    nsq[4:8, :] = jnp.zeros((4, 128), F32)
    rcopy(nsq, nr.at[0], ns, nrs, sib)
    for n, (dy, dx) in enumerate(offs):
        for kk in range(2):
            rcopy(nsq, nr.at[1 + 2 * n + kk], ns, nrs, plane(dy, dx, jnp.where(kk == 0, k, 1 - k)))

    for h in range(2):
        J = slice(256 * h, 256 * h + 256)
        K = 256 * (h + 1)
        a, b = lh[J, :K], ll[J, :K]
        orth = dot1(ph[:, :K], a, NT) + (dot1(ph[:, :K], b, NT) + dot1(plo[:, :K], a, NT))
        oh[:, J] = orth.astype(BF16)
        lf[:, J] = jnp.sqrt(F32(NZ * ROWS_L)) * orth
    for first in range(0, COLS_L, 256):
        cols = slice(first, min(first + 256, COLS_L))
        update = dot1(oh[...], bb[cols, :], NT)
        mn[:, cols] = (buf[:, cols].astype(F32) - F32(1.0 - decay) * update).astype(BF16)

    wait_for(nr.at[pl.ds(0, 31)], nrs)
    total = nsq[...]
    for n in range(31):
        total = total + nr[n]
    scale = jnp.sqrt(F32(2 * CHIPS * COLS_L)) * lax.rsqrt(total + 1e-06)
    for q in range(CH):
        J = slice(128 * q, 128 * q + 128)
        back[:, J] = back[:, J] * scale[q : q + 1, :]

    wait_for(nr.at[pl.ds(0, 31)], ns)
    for fn in finals:
        fn()


def finish(mom, left, right, mom_out, left_out, right_out, sems):
    pairs = [(right, right_out), (left, left_out), (mom, mom_out)]
    copies = [pltpu.make_async_copy(a, b, sems.at[n]) for n, (a, b) in enumerate(pairs)]
    for cp in copies:
        cp.start()
    for cp in copies:
        cp.wait()


def shards(momentum, gradient, basis):
    V = pltpu.VMEM
    D = pltpu.SemaphoreType.DMA
    scratch = [
        V((512, 896), BF16), V((512, 896), BF16), V((896, 512), BF16),
        V((512, 896), BF16), V((896, 512), BF16),
        V((CH, 512, 128), F32), V((CH, HALF, 128), F32), V((CH, CHIPS - 1, PIECE, 128), F32),
        V((CH, 512, 128), F32), V((512, 512), BF16), V((512, 512), BF16), V((CH, 896, 128), F32),
        V((CH, 2, 8, SH, 128), F32), V((CH, 2, 8, SH, 128), F32), V((CH, 896, 128), F32),
        V((896, 512), BF16), V((896, 512), BF16),
        V((OWN, 8, 128), F32), V((NZ, 8, 128), F32), V((TILES, 8, 128), F32),
        V((512, 512), F32), V((512, 512), F32), V((512, 512), F32), V((128, 128), F32),
        V((512, 512), BF16), V((512, 512), BF16), V((512, 512), BF16),
        V((896, 512), BF16), V((8, 128), F32), V((31, 8, 128), F32),
        D((3,)), D((CH,)), D((CH,)), D((CH,)), D((CH,)), D((CH,)), D((CH,)), D((CH,)), D((CH,)),
        D, D, D, D, D, D, D, D,
        D((CH, 2)), D((CH, 2, 8)), D((CH, 2, 8)), D((CH, 2, 8)), D((CH, 2, 8)), D, D,
    ]
    results = pl.pallas_call(
        kernel,
        name="dion",
        out_shape=(
            pltpu.VMEM((512, 896), BF16),
            pltpu.VMEM((512, 512), F32),
            pltpu.VMEM((896, 512), F32),
        ),
        in_specs=[pl.BlockSpec(memory_space=pltpu.HBM)] * 3,
        out_specs=[pl.BlockSpec(memory_space=pltpu.VMEM)] * 3,
        scratch_shapes=scratch,
        compiler_params=pltpu.CompilerParams(
            collective_id=0, has_side_effects=True, vmem_limit_bytes=40 * 2**20
        ),
    )(*[pltpu.with_memory_space_constraint(a, pltpu.HBM) for a in (momentum, gradient, basis)])
    return pl.pallas_call(
        finish,
        name="finish",
        out_shape=(
            jax.ShapeDtypeStruct((512, 896), BF16),
            jax.ShapeDtypeStruct((512, 512), F32),
            jax.ShapeDtypeStruct((896, 512), F32),
        ),
        in_specs=[pl.BlockSpec(memory_space=pl.ANY)] * 3,
        out_specs=[pl.BlockSpec(memory_space=pl.ANY)] * 3,
        scratch_shapes=[D((3,))],
        compiler_params=pltpu.CompilerParams(vmem_limit_bytes=4 * 2**20),
    )(*results)


def solution(mesh):
    in_specs = (P("row", "col"), P("row", "col"), P("col", None))
    out_specs = (P("row", "col"), P("row", None), P("col", None))
    return jax.shard_map(shards, mesh=mesh, in_specs=in_specs, out_specs=out_specs, check_vma=False)
```

time: 120 us -> 101 us (0.84)
  Pallas kernels: 112 us -> 99.7 us
  local copies, waits for them, and re-layouts: 7.27 us -> 0 us
    pallas_call x1 -> x2, Pallas kernels: 112 us -> 99.7 us  [the longest x1 97.8 us: shards(): pl.pallas_call(kernel, name='dion', out_shape=(pltpu.VMEM((512, 896), BF1...]
    unnamed x13 -> x0, local copies, waits for them, and re-layouts: 7.27 us -> none
where the time goes in v2:
time: 101 us
  Pallas kernels  99.7 us (99%)
    pallas_call x1, Pallas kernels, shards(): pl.pallas_call(kernel, name='dion', out_shape=(pltpu.VMEM((512, 896), BF1...  97.8 us

profile of v2, /device:TPU:1, one launch (start us, length us, event | category | flops | bytes accessed | tf_op | source)
XLA Modules:
  0.0 100.6 jit_solution(1202486923644064365)
XLA Ops:
  0.6 97.8 %dion.1 = (bf16[512,896]{1,0:T(8,128)(2,1)S(1)}, f32[512,512]{1,0:T(8,128)S(1)}, f32[896,512]{1,0:T(8,128)S(1)}) custom-call(bf16[512,896]{1,0:T(8,128)(2,1)} %m_hbm.1, bf16[512,896]{1,0:T(8,128)(2,1)} %g_hbm.1, bf16[896,512]{1,0:T(8,128)(2,1)} %q_hbm.1), custom_call_target="tpu_custom_call" | custom-call | tf_op jit(solution)/shard_map/dion/pallas_call | solution.py:487
  98.5 1.9 %finish.1 = (bf16[512,896]{1,0:T(8,128)(2,1)}, f32[512,512]{1,0:T(8,128)}, f32[896,512]{1,0:T(8,128)}) custom-call(bf16[512,896]{1,0:T(8,128)(2,1)S(1)} %get-tuple-element.6.mom, f32[512,512]{1,0:T(8,128)S(1)} %get-tuple-element.7.left, f32[896,512]{1,0:T(8,128)S(1)} %get-tuple-element.8.right), custom_call_target="tpu_custom_call" | custom-call | tf_op jit(solution)/shard_map/finish/pallas_call | solution.py:502

commit v3 on v2

--- a/solution.py
+++ b/solution.py
@@ -28,6 +28,8 @@
     ((7, 6, 5, 4, 3, 2, 1, 0), (8, 7, 6, 5, 4, 3, 2, 0)),
 ]
 SOLO_AT = 2
+NORM_GAPS = 6
+HEAD_AT = (3, 9)
 GRAM_AT = (8, 14, 21, 24)
 PER_GAP = 3
 NN = ((1,), (0,))
@@ -98,9 +100,9 @@
 def kernel(
     m_hbm, g_hbm, q_hbm, mn, lf, back,
     mv, gv, qv, buf, mt, pp, sibr, rsr, pf, ph, plo, bp,
-    run, solo, bfull, bh, bl, gl, gr, gt, pt, g, li, wd, lh, ll, oh, bb, nsq, nr,
+    run, solo, bfull, bh, bl, gl, gr, gt, ha, hp, ht, pt, g, li, wd, lh, ll, oh, bb, nsq, nr, nt, nz,
     in_s, s1s, s1r, s2s, s2r, s3s, s3r, s4s, s4r,
-    gzs, gzr, gbs, gbr, gps, gpr, gss, gsr,
+    gzs, gzr, gbs, gbr, gps, gpr, gss, gsr, has, har, hbs, hbr, nzs, nzr,
     ring_s, run_r, solo_r, all_r, skip_r, ns, nrs,
 ):
     z = lax.axis_index("row")
@@ -299,11 +301,58 @@
         events.append(ring_events(q))
         next(events[q])
         pt[cols, :] = pf[q].T
+        if q == 0:
+            @pl.when(k == 0)
+            def _():
+                ha[...] = doth(pt[pl.ds(pl.multiple_of(8 * chip, 8), 8), :], pf[0], NN)
+                for dz in range(1, NZ):
+                    rcopy(ha, hp.at[z], has, har, dev((z + dz) % NZ, y, x, k))
 
     my_u = (z % 8) * 3 % 8
     owner = my_u < OWN
     my_u = my_u % OWN
     my_tiles = OWN * mine
+
+    eye = lax.broadcasted_iota(jnp.int32, (128, 128), 0) == lax.broadcasted_iota(jnp.int32, (128, 128), 1)
+
+    def head():
+        @pl.when(k == 0)
+        def _():
+            wait_for(hp.at[pl.ds(0, NZ - 1)], har)
+            hp[z] = ha[...]
+            total = hp[0]
+            for n in range(1, NZ):
+                total = total + hp[n]
+            ht[chip] = total
+            tile = ht.at[chip]
+            rcopy(tile, tile, hbs, hbr, sib)
+            for dy, dx in offs:
+                for kk in range(2):
+                    rcopy(tile, tile, hbs, hbr, plane(dy, dx, kk))
+
+        def done_sending():
+            @pl.when(k == 0)
+            def _():
+                wait_for(gt.at[pl.ds(0, NZ - 1)], has)
+                wait_for(gt.at[pl.ds(0, 31)], hbs)
+
+        finals.append(done_sending)
+        yield
+
+        @pl.when(k == 0)
+        def _():
+            wait_for(gt.at[pl.ds(0, CHIPS - 1)], hbr)
+
+        @pl.when(k == 1)
+        def _():
+            wait_for(gt.at[pl.ds(0, CHIPS)], hbr)
+
+        g[:128, :128] = ht[...].reshape(128, 128)
+        wd[...] = eye.astype(F32)
+        yield
+        for t in range(16):
+            leaf(g.at[:128, :128], wd, t)
+            yield
 
     def chol():
         for u in range(OWN):
@@ -362,17 +411,18 @@
         rcopy(half, half, gss, gsr, sib)
         yield
         wait_for(gt.at[pl.ds(0, OWN * CHIPS)], gsr)
-        for b, (i, j) in enumerate(BLOCKS):
+        for b, (i, j) in enumerate(BLOCKS[1:], 1):
             g[128 * i : 128 * i + 128, 128 * j : 128 * j + 128] = gt[16 * b : 16 * b + 16].reshape(128, 128)
         yield
-        eye = lax.broadcasted_iota(jnp.int32, (128, 128), 0) == lax.broadcasted_iota(jnp.int32, (128, 128), 1)
+        yield from first
         for kb in range(4):
             K = slice(128 * kb, 128 * kb + 128)
             before = slice(0, 128 * kb)
-            wd[...] = eye.astype(F32)
-            for t in range(16):
-                leaf(g.at[K, K], wd, t)
-                yield
+            if kb:
+                wd[...] = eye.astype(F32)
+                for t in range(16):
+                    leaf(g.at[K, K], wd, t)
+                    yield
             w = wd[...]
             li[K, K] = w
             if kb:
@@ -388,8 +438,39 @@
                 li[K, 128 * (kb + 1) :] = jnp.zeros((128, 512 - 128 * (kb + 1)), F32)
             yield
         lh[...], ll[...] = split(li[...])
-        yield
-
+        own = pl.ds(pl.multiple_of(SH * z, 8), SH)
+        high, low = split(jnp.concatenate([bfull[q, own, :] for q in range(CH)], axis=1))
+        part = dot1(high, lh[...], NT) + (dot1(high, ll[...], NT) + dot1(low, lh[...], NT))
+        sq = jnp.sum(part * part, axis=0, keepdims=True)
+        for q in range(CH):
+            nsq[q : q + 1, :] = sq[:, 128 * q : 128 * q + 128]
+        finals.append(lambda: wait_for(nr, ns))
+        rcopy(nsq, nr.at[0], ns, nrs, sib)
+        for n, (dy, dx) in enumerate(offs):
+            for kk in range(2):
+                rcopy(nsq, nr.at[1 + 2 * n + kk], ns, nrs, plane(dy, dx, jnp.where(kk == 0, k, 1 - k)))
+        yield
+        for h in range(2):
+            J = slice(256 * h, 256 * h + 256)
+            K = 256 * (h + 1)
+            a, b = lh[J, :K], ll[J, :K]
+            orth = dot1(ph[:, :K], a, NT) + (dot1(ph[:, :K], b, NT) + dot1(plo[:, :K], a, NT))
+            oh[:, J] = orth.astype(BF16)
+            lf[:, J] = jnp.sqrt(F32(NZ * ROWS_L)) * orth
+            yield
+        for _ in range(PER_GAP * NORM_GAPS - 2):
+            yield
+        wait_for(nr, nrs)
+        total = nsq[...]
+        for n in range(31):
+            total = total + nr[n]
+        nt[...] = total
+        finals.append(lambda: wait_for(nz.at[pl.ds(0, NZ - 1)], nzs))
+        for dz in range(1, NZ):
+            rcopy(nt, nz.at[z], nzs, nzr, dev((z + dz) % NZ, y, x, k))
+        yield
+
+    first = head()
     work = chol()
     done = object()
 
@@ -409,6 +490,8 @@
                 pull(1)
             elif count > GRAM_AT[-1]:
                 pull(PER_GAP)
+            if count in HEAD_AT or HEAD_AT[-1] < count < GRAM_AT[-1]:
+                next(first, done)
     while next(work, done) is not done:
         pass
 
@@ -422,37 +505,21 @@
         part = dot1(bh[:, :K], a, NT) + (dot1(bh[:, :K], b, NT) + dot1(bl[:, :K], a, NT))
         back[:, J] = part
         bb[:, J] = part.astype(BF16)
-        sq = jnp.sum(part * part, axis=0, keepdims=True)
-        nsq[2 * h : 2 * h + 1, :] = sq[:, :128]
-        nsq[2 * h + 1 : 2 * h + 2, :] = sq[:, 128:]
-    nsq[4:8, :] = jnp.zeros((4, 128), F32)
-    rcopy(nsq, nr.at[0], ns, nrs, sib)
-    for n, (dy, dx) in enumerate(offs):
-        for kk in range(2):
-            rcopy(nsq, nr.at[1 + 2 * n + kk], ns, nrs, plane(dy, dx, jnp.where(kk == 0, k, 1 - k)))
-
-    for h in range(2):
-        J = slice(256 * h, 256 * h + 256)
-        K = 256 * (h + 1)
-        a, b = lh[J, :K], ll[J, :K]
-        orth = dot1(ph[:, :K], a, NT) + (dot1(ph[:, :K], b, NT) + dot1(plo[:, :K], a, NT))
-        oh[:, J] = orth.astype(BF16)
-        lf[:, J] = jnp.sqrt(F32(NZ * ROWS_L)) * orth
     for first in range(0, COLS_L, 256):
         cols = slice(first, min(first + 256, COLS_L))
         update = dot1(oh[...], bb[cols, :], NT)
         mn[:, cols] = (buf[:, cols].astype(F32) - F32(1.0 - decay) * update).astype(BF16)
 
-    wait_for(nr.at[pl.ds(0, 31)], nrs)
-    total = nsq[...]
-    for n in range(31):
-        total = total + nr[n]
+    wait_for(nz.at[pl.ds(0, NZ - 1)], nzr)
+    nz[z] = nt[...]
+    total = nz[0]
+    for n in range(1, NZ):
+        total = total + nz[n]
     scale = jnp.sqrt(F32(2 * CHIPS * COLS_L)) * lax.rsqrt(total + 1e-06)
     for q in range(CH):
         J = slice(128 * q, 128 * q + 128)
         back[:, J] = back[:, J] * scale[q : q + 1, :]
 
-    wait_for(nr.at[pl.ds(0, 31)], ns)
     for fn in finals:
         fn()
 
@@ -477,11 +544,12 @@
         V((CH, 2, 8, SH, 128), F32), V((CH, 2, 8, SH, 128), F32), V((CH, 896, 128), F32),
         V((896, 512), BF16), V((896, 512), BF16),
         V((OWN, 8, 128), F32), V((NZ, 8, 128), F32), V((TILES, 8, 128), F32),
+        V((8, 128), F32), V((NZ, 8, 128), F32), V((16, 8, 128), F32),
         V((512, 512), F32), V((512, 512), F32), V((512, 512), F32), V((128, 128), F32),
         V((512, 512), BF16), V((512, 512), BF16), V((512, 512), BF16),
-        V((896, 512), BF16), V((8, 128), F32), V((31, 8, 128), F32),
+        V((896, 512), BF16), V((4, 128), F32), V((31, 4, 128), F32), V((4, 128), F32), V((NZ, 4, 128), F32),
         D((3,)), D((CH,)), D((CH,)), D((CH,)), D((CH,)), D((CH,)), D((CH,)), D((CH,)), D((CH,)),
-        D, D, D, D, D, D, D, D,
+        D, D, D, D, D, D, D, D, D, D, D, D, D, D,
         D((CH, 2)), D((CH, 2, 8)), D((CH, 2, 8)), D((CH, 2, 8)), D((CH, 2, 8)), D, D,
     ]
     results = pl.pallas_call(

time: 101 us -> 97.9 us (0.969)
  Pallas kernels: 99.7 us -> 96.9 us
    pallas_call x1, Pallas kernels: 97.8 us -> 95 us  [shards(): pl.pallas_call(kernel, name='dion', out_shape=(pltpu.VMEM((512, 896), BF1...]
where the time goes in v3:
time: 97.9 us; the launch traced here: 97.7 us
  Pallas kernels  96.9 us (99%)
    pallas_call x1, Pallas kernels, shards(): pl.pallas_call(kernel, name='dion', out_shape=(pltpu.VMEM((512, 896), BF1...  95 us

profile of v3, /device:TPU:1, one launch (start us, length us, event | category | flops | bytes accessed | tf_op | source)
XLA Modules:
  0.0 97.7 jit_solution(15325086754417147749)
XLA Ops:
  0.6 95.0 %dion.1 = (bf16[512,896]{1,0:T(8,128)(2,1)S(1)}, f32[512,512]{1,0:T(8,128)S(1)}, f32[896,512]{1,0:T(8,128)S(1)}) custom-call(bf16[512,896]{1,0:T(8,128)(2,1)} %m_hbm.1, bf16[512,896]{1,0:T(8,128)(2,1)} %g_hbm.1, bf16[896,512]{1,0:T(8,128)(2,1)} %q_hbm.1), custom_call_target="tpu_custom_call" | custom-call | tf_op jit(solution)/shard_map/dion/pallas_call | solution.py:555
  95.6 1.9 %finish.1 = (bf16[512,896]{1,0:T(8,128)(2,1)}, f32[512,512]{1,0:T(8,128)}, f32[896,512]{1,0:T(8,128)}) custom-call(bf16[512,896]{1,0:T(8,128)(2,1)S(1)} %get-tuple-element.6.mom, f32[512,512]{1,0:T(8,128)S(1)} %get-tuple-element.7.left, f32[896,512]{1,0:T(8,128)S(1)} %get-tuple-element.8.right), custom_call_target="tpu_custom_call" | custom-call | tf_op jit(solution)/shard_map/finish/pallas_call | solution.py:570

commit v4 on v3

--- a/solution.py
+++ b/solution.py
@@ -27,7 +27,6 @@
     ((8, 7, 6, 5, 4, 3, 2, 0), (7, 6, 5, 4, 3, 2, 1, 0)),
     ((7, 6, 5, 4, 3, 2, 1, 0), (8, 7, 6, 5, 4, 3, 2, 0)),
 ]
-SOLO_AT = 2
 NORM_GAPS = 6
 HEAD_AT = (3, 9)
 GRAM_AT = (8, 14, 21, 24)
@@ -232,8 +231,6 @@
                     if stops[i] - stops[i + 1] == 2:
                         send(bp.at[q, at(way, stops[i] - 1)], solo.at[q, way, i], way, solo_r.at[q, way, i], 1)
 
-        if SOLO_AT == 0:
-            solos()
         yield
 
         def arrived(way, i):
@@ -251,7 +248,7 @@
                 if i < hops[way]:
                     run[q, way, i - 1] = arrived(way, i - 1) + bp[q, at(way, stops[i]), :]
                     send(run.at[q, way, i - 1], run.at[q, way, i], way, run_r.at[q, way, i], stops[i] - stops[i + 1])
-            if i == SOLO_AT:
+            if i == 1 + q:
                 solos()
             yield
         own = shard(z)
@@ -277,7 +274,7 @@
                 if i <= hops[way]:
                     forward(way, i)
             for way in range(2):
-                skips(way, i - 1)
+                skips(way, i - 1 - q)
             if i == max(hops):
                 for way in range(2):
                     stops = PLANS[q][way][::-1]
@@ -479,10 +476,31 @@
             next(work, done)
 
     pull(1)
+    def products(rows, cols):
+        for q in range(cols.start // LW, cols.stop // LW):
+            J = slice(LW * q, LW * q + LW)
+            bh[:, J], bl[:, J] = split(bfull[q])
+        a, b = lh[rows, cols], ll[rows, cols]
+        return dot1(bh[:, cols], a, NT) + (dot1(bh[:, cols], b, NT) + dot1(bl[:, cols], a, NT))
+
+    def apply_early():
+        while next(work, done) is not done:
+            pass
+        part = products(slice(0, 512), slice(0, 256))
+        back[...] = part
+        bb[:, :256] = part[:, :256].astype(BF16)
+
+    def apply_late():
+        part = back[:, 256:] + products(slice(256, 512), slice(256, 512))
+        back[:, 256:] = part
+        bb[:, 256:] = part.astype(BF16)
+
     last = max(len(p) - 1 for plan in PLANS for p in plan) * 2
     count = 0
     for e in range(1, last + 1):
         for q in range(CH):
+            if e == last and q == 2:
+                apply_early()
             if next(events[q], done) is done:
                 continue
             count += 1
@@ -492,19 +510,7 @@
                 pull(PER_GAP)
             if count in HEAD_AT or HEAD_AT[-1] < count < GRAM_AT[-1]:
                 next(first, done)
-    while next(work, done) is not done:
-        pass
-
-    for q in range(CH):
-        J = slice(128 * q, 128 * q + 128)
-        bh[:, J], bl[:, J] = split(bfull[q])
-    for h in range(2):
-        J = slice(256 * h, 256 * h + 256)
-        K = 256 * (h + 1)
-        a, b = lh[J, :K], ll[J, :K]
-        part = dot1(bh[:, :K], a, NT) + (dot1(bh[:, :K], b, NT) + dot1(bl[:, :K], a, NT))
-        back[:, J] = part
-        bb[:, J] = part.astype(BF16)
+    apply_late()
     for first in range(0, COLS_L, 256):
         cols = slice(first, min(first + 256, COLS_L))
         update = dot1(oh[...], bb[cols, :], NT)

time: 97.9 us -> 97.8 us (level)
  no operation moved by 1% of the time
where the time goes in v4:
time: 97.8 us; the launch traced here: 97.6 us
  Pallas kernels  96.7 us (99%)
    pallas_call x1, Pallas kernels, shards(): pl.pallas_call(kernel, name='dion', out_shape=(pltpu.VMEM((512, 896), BF1...  94.8 us

profile of v4, /device:TPU:1, one launch (start us, length us, event | category | flops | bytes accessed | tf_op | source)
XLA Modules:
  0.0 97.6 jit_solution(13586896956292822316)
XLA Ops:
  0.6 94.8 %dion.1 = (bf16[512,896]{1,0:T(8,128)(2,1)S(1)}, f32[512,512]{1,0:T(8,128)S(1)}, f32[896,512]{1,0:T(8,128)S(1)}) custom-call(bf16[512,896]{1,0:T(8,128)(2,1)} %m_hbm.1, bf16[512,896]{1,0:T(8,128)(2,1)} %g_hbm.1, bf16[896,512]{1,0:T(8,128)(2,1)} %q_hbm.1), custom_call_target="tpu_custom_call" | custom-call | tf_op jit(solution)/shard_map/dion/pallas_call | solution.py:561
  95.5 1.9 %finish.1 = (bf16[512,896]{1,0:T(8,128)(2,1)}, f32[512,512]{1,0:T(8,128)}, f32[896,512]{1,0:T(8,128)}) custom-call(bf16[512,896]{1,0:T(8,128)(2,1)S(1)} %get-tuple-element.6.mom, f32[512,512]{1,0:T(8,128)S(1)} %get-tuple-element.7.left, f32[896,512]{1,0:T(8,128)S(1)} %get-tuple-element.8.right), custom_call_target="tpu_custom_call" | custom-call | tf_op jit(solution)/shard_map/finish/pallas_call | solution.py:576
